TPU v7x, 32 devices: a whole 2x2x4 slice. The times are simulated.
32 devices in a mesh: groups: 2 (over y), dp: 4 (over z), section: 4 (over x, core).
Axes of the slice: x: 2, y: 2, z: 4, core: 2. Of those that a mesh axis runs over, the one named last changes fastest.
Arguments:
- images: bfloat16 [4, 8, 16, 5120], P(None, ('groups', 'dp')), parts along dimension 1, may hold values from -40 to 40
- cotangent: bfloat16 [4, 8, 16, 5120], P(None, ('groups', 'dp')), parts along dimension 1, may hold values from -6 to 6
- in_weight: bfloat16 [4, 1280, 320], P('section'), may hold values from -0.3125 to 0.3125
- out_weight: bfloat16 [4, 1280, 320], P('section'), may hold values from -0.15625 to 0.15625
- depth_kernel: float32 [4, 49, 320], P('section'), may hold values from -0.875 to 0.875
- norm_gain: float32 [4, 320], P('section'), may hold values from 0.1 to 1.9
Outputs:
- input_grads: bfloat16 [4, 4, 8, 16, 5120], P('section', None, ('groups', 'dp')), parts along dimension 2
- in_weight_grad: float32 [8, 1280, 320], P(('groups', 'section'), 'dp'), parts along dimension 0
- out_weight_grad: float32 [8, 1280, 320], P(('groups', 'section'), 'dp'), parts along dimension 0
- kernel_grad: float32 [8, 49, 320], P(('groups', 'section')), parts along dimension 0
- gain_grad: float32 [8, 320], P(('groups', 'section')), parts along dimension 0
There are 2 independent parts, one for each index of `groups`. A program takes and returns all parts, laid end to end along the dimension named above; an argument that names none is the same for every part. Nothing has to cross between parts.
All inputs are finite; a program needn't handle non-finite values.
Results may differ from a plain program's by a relative error of at most 0.015.
Values may be sent and summed in bfloat16 or wider, within the bound.
A program may use at most 64 MiB of HBM per device.

v0:
```python
import functools

import jax
import jax.numpy as jnp
from jax import lax
from jax.experimental import pallas as pl
from jax.experimental.pallas import tpu as pltpu
from jax.sharding import PartitionSpec as P

KS = 7
REACH = KS // 2
LANES = 128
MESH = pl.DeviceIdType.MESH

gelu_scale = 0.7978845608028654
cubic_term = 0.044715
norm_eps = 1e-06
F32 = jnp.float32
BF16 = jnp.bfloat16


def half_turn(tile):
    return pltpu.roll(tile, LANES // 2, axis=tile.ndim - 1)


def low_lanes(tile):
    return lax.broadcasted_iota(jnp.int32, tile.shape, tile.ndim - 1) < LANES // 2


def split_pair(tiles):
    t0, t1, t2, t3, t4 = tiles
    low = low_lanes(t0)
    q2, q3, q4 = half_turn(t2), half_turn(t3), half_turn(t4)
    first = (t0, t1, jnp.where(low, t2, 0.0))
    second = (jnp.where(low, q2, q3), jnp.where(low, q3, q4), jnp.where(low, q4, 0.0))
    return first, second


def merge_pair(first, second):
    low = low_lanes(first[0])
    q0, q1, q2 = (half_turn(t) for t in second)
    return (
        first[0],
        first[1],
        jnp.where(low, first[2], q0),
        jnp.where(low, q0, q1),
        jnp.where(low, q1, q2),
    )


def lane_tiles(value):
    return tuple(value[:, k * LANES : (k + 1) * LANES] for k in range(value.shape[1] // LANES))


def from_native(ref, slot):
    rows, width = ref.shape[1], ref.shape[2]
    parts = []
    for pair in range(width // (5 * LANES)):
        value = ref[slot, :, pair * 5 * LANES : (pair + 1) * 5 * LANES].astype(F32)
        first, second = split_pair(lane_tiles(value))
        parts.append(jnp.concatenate(first, axis=1))
        parts.append(jnp.concatenate(second, axis=1))
    return jnp.concatenate(parts, axis=0)


def to_native(ref, slot, value):
    rows, width = ref.shape[1], ref.shape[2]
    for pair in range(width // (5 * LANES)):
        first = lane_tiles(value[2 * pair * rows : (2 * pair + 1) * rows])
        second = lane_tiles(value[(2 * pair + 1) * rows : (2 * pair + 2) * rows])
        for k, tile in enumerate(merge_pair(first, second)):
            at = (pair * 5 + k) * LANES
            ref[slot, :, at : at + LANES] = tile.astype(ref.dtype)


def put_padded(field, slot, value, rows):
    half = value.shape[0] // 2
    pairs = half // rows
    left, right = lane_tiles(value[:half]), lane_tiles(value[half:])
    body = merge_pair(left, right)
    edge = REACH * rows
    zeros = tuple(jnp.zeros((edge, LANES), F32) for _ in range(3))
    before = merge_pair(zeros, lane_tiles(value[half - edge : half]))
    after = lane_tiles(value[half : half + edge])
    for k in range(5):
        field[slot, k, REACH : REACH + pairs, 8 : 8 + rows, :] = body[k].reshape(pairs, rows, LANES)
        if k >= 2:
            field[slot, k, 0:REACH, 8 : 8 + rows, :] = before[k].reshape(REACH, rows, LANES)
        if k <= 2:
            field[slot, k, REACH + pairs :, 8 : 8 + rows, :] = after[k].reshape(REACH, rows, LANES)
    return body


def convolve(field, slot, taps, out, flip):
    pairs, rows = out.shape[1], out.shape[2]

    def one_tile(k, carry):
        for part in range(rows // 8):
            total = jnp.zeros((pairs, 8, LANES), F32)
            for i in range(KS):
                window = field[slot, k, :, 8 - REACH + i + 8 * part : 16 - REACH + i + 8 * part, :]
                for j in range(KS):
                    tap = KS * i + j
                    tap = KS * KS - 1 - tap if flip else tap
                    total = total + window[j : j + pairs] * taps[k, tap][None]
            out[k, :, 8 * part : 8 * part + 8, :] = total
        return carry

    lax.fori_loop(0, 5, one_tile, 0)
    tiles = tuple(out[k].reshape(pairs * rows, LANES) for k in range(5))
    first, second = split_pair(tiles)
    return jnp.concatenate(
        [jnp.concatenate(first, axis=1), jnp.concatenate(second, axis=1)], axis=0
    )


def tap_terms(field, slot, kept, sums):
    pairs, rows = kept.shape[2], kept.shape[3]

    def one_tile(k, carry):
        for i in range(KS):
            windows = [
                field[slot, k, :, 8 - REACH + i + 8 * part : 16 - REACH + i + 8 * part, :]
                for part in range(rows // 8)
            ]
            for j in range(KS):
                total = None
                for part in range(rows // 8):
                    term = jnp.sum(
                        windows[part][j : j + pairs]
                        * kept[slot, k, :, 8 * part : 8 * part + 8, :],
                        axis=0,
                    )
                    total = term if total is None else total + term
                tap = KS * KS - 1 - (KS * i + j)
                sums[k, tap] = sums[k, tap] + total
        return carry

    lax.fori_loop(0, 5, one_tile, 0)


def step_kernel(
    sections, replicas, spread, channels, mean_scale,
    images, cotangent, weight_in, weight_out, kernel, gain,
    stored, in_grad, out_grad, kernel_grad, gain_grad,
    x_in, x_out, g_in, win, wout, taps, wide, gain_wide,
    hidden, slope, act_grad, normed, upstream, unit, inv_std,
    field, kept, conv, tap_sums, gain_sums, sent, landed, small, small_in,
    load_sem, fwd_send, fwd_recv, bwd_send, bwd_recv, sum_send, sum_recv, small_send, small_recv,
):
    me = lax.axis_index("section")
    replica = lax.axis_index("dp")
    last = sections - 1
    micro_count, rows, width = x_in.shape
    hidden_width = weight_in.shape[0]
    step = 256
    chunks = hidden_width // step
    pixels = rows * (width // channels)

    barrier = pltpu.get_barrier_semaphore()

    @pl.when(me > 0)
    def _():
        pl.semaphore_signal(barrier, inc=1, device_id={"section": me - 1}, device_id_type=MESH)

    @pl.when(me < last)
    def _():
        pl.semaphore_signal(barrier, inc=1, device_id={"section": me + 1}, device_id_type=MESH)

    if spread:
        for k in range(1, replicas):
            pl.semaphore_signal(
                barrier, inc=1,
                device_id={"dp": lax.rem(replica + k, replicas)}, device_id_type=MESH,
            )

    def load(source, target, m, which):
        return pltpu.make_async_copy(source.at[m], target.at[m], load_sem.at[which, m])

    for m in range(micro_count):
        @pl.when(me == 0)
        def _():
            load(images, x_in, m, 0).start()

        @pl.when(me == last)
        def _():
            load(cotangent, g_in, m, 1).start()

    win[:, 256:384] = jnp.zeros((hidden_width, 128), BF16)
    wout[:, 256:384] = jnp.zeros((hidden_width, 128), BF16)
    win[:, 0:channels] = weight_in[...]
    wout[:, 0:channels] = weight_out[...]
    wide[...] = jnp.zeros(wide.shape, F32)
    gain_wide[...] = jnp.zeros(gain_wide.shape, F32)
    wide[0 : KS * KS, 0:channels] = kernel[...]
    gain_wide[:, 0:channels] = jnp.broadcast_to(gain[...], (8, channels))
    row_tiles = lane_tiles(wide[...])
    for k, tile in enumerate(merge_pair(row_tiles, row_tiles)):
        for t in range(KS * KS):
            taps[k, t] = jnp.broadcast_to(tile[t : t + 1], (8, LANES))
    field[...] = jnp.zeros(field.shape, F32)
    tap_sums[...] = jnp.zeros(tap_sums.shape, F32)
    gain_sums[...] = jnp.zeros(gain_sums.shape, F32)
    gain_row = gain_wide[0:1, :]

    neighbours = jnp.where(me > 0, 1, 0) + jnp.where(me < last, 1, 0)
    if spread:
        neighbours = neighbours + replicas - 1
    pl.semaphore_wait(barrier, neighbours)

    real = lax.broadcasted_iota(jnp.int32, (pixels, 384), 1) < channels
    by_channel = (((1,), (1,)), ((), ()))
    by_pixel = (((0,), (0,)), ((), ()))

    def ahead(m):
        return pltpu.make_async_remote_copy(
            src_ref=x_out.at[m], dst_ref=x_in.at[m],
            send_sem=fwd_send.at[m], recv_sem=fwd_recv.at[m],
            device_id={"section": jnp.minimum(me + 1, last)}, device_id_type=MESH,
        )

    def back(m):
        return pltpu.make_async_remote_copy(
            src_ref=stored.at[m], dst_ref=g_in.at[m],
            send_sem=bwd_send.at[m], recv_sem=bwd_recv.at[m],
            device_id={"section": jnp.maximum(me - 1, 0)}, device_id_type=MESH,
        )

    def forward(m, carry):
        @pl.when(me == 0)
        def _():
            load(images, x_in, m, 0).wait()

        @pl.when(me > 0)
        def _():
            ahead(m).wait_recv()

        x = from_native(x_in, m)
        body = put_padded(field, m, x, rows)
        for k in range(5):
            kept[m, k] = body[k].reshape(kept.shape[2:])
        u = convolve(field, m, taps, conv, False)
        mean = jnp.sum(u, axis=1, keepdims=True) * (1.0 / channels)
        centred = jnp.where(real, u - mean, 0.0)
        variance = jnp.sum(centred * centred, axis=1, keepdims=True) * (1.0 / channels)
        inverse = lax.rsqrt(variance + norm_eps)
        nhat = centred * inverse
        unit[m] = nhat
        inv_std[m] = jnp.broadcast_to(inverse, (pixels, LANES))
        n = (nhat * gain_row).astype(BF16)
        normed[m] = n
        mixed = None
        for c in range(chunks):
            at = slice(c * step, (c + 1) * step)
            a = lax.dot_general(n, win[at, :], by_channel, preferred_element_type=F32)
            square = a * a
            t = jnp.tanh(a * (gelu_scale + (gelu_scale * cubic_term) * square))
            plus = 0.5 + 0.5 * t
            h = (a * plus).astype(BF16)
            hidden[m, :, at] = h
            slope[m, :, at] = plus + (a * (plus * (1.0 - t))) * (
                gelu_scale + (3.0 * gelu_scale * cubic_term) * square
            )
            term = jnp.dot(h, wout[at, :], preferred_element_type=F32)
            mixed = term if mixed is None else mixed + term

        @pl.when(me < last)
        def _():
            to_native(x_out, m, x + mixed)
            ahead(m).start()

        return carry

    lax.fori_loop(0, micro_count, forward, 0)

    def backward(m, carry):
        @pl.when(me == last)
        def _():
            load(cotangent, g_in, m, 1).wait()

        @pl.when(me < last)
        def _():
            back(m).wait_recv()

        g = from_native(g_in, m)
        gb = g.astype(BF16)
        upstream[m] = gb
        dn = None
        for c in range(chunks):
            at = slice(c * step, (c + 1) * step)
            hg = lax.dot_general(gb, wout[at, :], by_channel, preferred_element_type=F32)
            da = (hg * slope[m, :, at]).astype(BF16)
            act_grad[m, :, at] = da
            term = jnp.dot(da, win[at, :], preferred_element_type=F32)
            dn = term if dn is None else dn + term
        nhat = unit[m]
        along = dn * nhat
        gain_sums[...] = gain_sums[...] + jnp.sum(along.reshape(pixels // 8, 8, 384), axis=0)
        q = dn * gain_row
        first = jnp.sum(q, axis=1, keepdims=True) * (1.0 / channels)
        second = jnp.sum(along * gain_row, axis=1, keepdims=True) * (1.0 / channels)
        du = jnp.where(real, inv_std[m][:, 0:1] * (q - first - nhat * second), 0.0)
        put_padded(field, m, du, rows)
        to_native(stored, m, g + convolve(field, m, taps, conv, True))

        @pl.when(me > 0)
        def _():
            back(m).start()

        return carry

    lax.fori_loop(0, micro_count, backward, 0)

    def share(w, k):
        chunk = hidden_width // replicas
        dest = lax.rem(replica + k, replicas)
        return pltpu.make_async_remote_copy(
            src_ref=sent.at[w, pl.ds(pl.multiple_of(dest * chunk, 16), chunk), :],
            dst_ref=landed.at[w, k - 1],
            send_sem=sum_send.at[w, k - 1], recv_sem=sum_recv.at[w, k - 1],
            device_id={"dp": dest}, device_id_type=MESH,
        )

    for w, (wide_side, thin_side) in enumerate(((hidden, upstream), (act_grad, normed))):
        for c in range(chunks):
            at = slice(c * step, (c + 1) * step)
            total = lax.dot_general(
                wide_side[:, :, at].reshape(micro_count * pixels, step),
                thin_side[...].reshape(micro_count * pixels, 384),
                by_pixel, preferred_element_type=F32,
            )
            total = (total[:, 0:channels] * mean_scale).astype(BF16)
            if spread:
                sent[w, at, :] = total
            elif w == 0:
                out_grad[at, :] = total
            else:
                in_grad[at, :] = total
        if spread:
            for k in range(1, replicas):
                share(w, k).start()

    def per_micro(m, carry):
        tap_terms(field, m, kept, tap_sums)
        return carry

    lax.fori_loop(0, micro_count, per_micro, 0)

    sums = tuple(jnp.sum(tap_sums[k], axis=1) for k in range(5))
    first, second = split_pair(sums)
    both = (jnp.concatenate(first, axis=1) + jnp.concatenate(second, axis=1)) * mean_scale
    gains = jnp.sum(gain_sums[...], axis=0, keepdims=True) * mean_scale
    if not spread:
        kernel_grad[...] = both[:, 0:channels]
        gain_grad[...] = gains[:, 0:channels]
    else:
        small[...] = jnp.zeros(small.shape, BF16)
        small[0:64, :] = jnp.concatenate(
            [both, jnp.zeros((15, 384), F32)], axis=0
        ).astype(BF16)
        small[64:80, :] = jnp.broadcast_to(gains, (16, 384)).astype(BF16)

        def share_small(k):
            return pltpu.make_async_remote_copy(
                src_ref=small, dst_ref=small_in.at[replica],
                send_sem=small_send.at[k - 1], recv_sem=small_recv.at[k - 1],
                device_id={"dp": lax.rem(replica + k, replicas)}, device_id_type=MESH,
            )

        for k in range(1, replicas):
            share_small(k).start()
        small_in[replica] = small[...]
        chunk = hidden_width // replicas
        mine = pl.ds(pl.multiple_of(replica * chunk, 16), chunk)
        for w, target in ((0, out_grad), (1, in_grad)):
            for k in range(1, replicas):
                share(w, k).wait()
            total = sent[w, mine, :].astype(F32)
            for k in range(1, replicas):
                total = total + landed[w, k - 1].astype(F32)
            target[...] = total
        for k in range(1, replicas):
            share_small(k).wait()
        total = small_in[0].astype(F32)
        for k in range(1, replicas):
            total = total + small_in[k].astype(F32)
        kernel_grad[...] = total[0 : KS * KS, 0:channels]
        gain_grad[...] = total[64:65, 0:channels]

    def drain(m, carry):
        @pl.when(me < last)
        def _():
            ahead(m).wait_send()

        @pl.when(me > 0)
        def _():
            back(m).wait_send()

        return carry

    lax.fori_loop(0, micro_count, drain, 0)


def local(images, cotangent, in_weight, out_weight, depth_kernel, norm_gain):
    sections = lax.axis_size("section")
    replicas = lax.axis_size("dp")
    micro_count, batch, rows, width = images.shape
    hidden_width, channels = in_weight.shape[1:]
    columns = width // channels
    pixels = rows * columns
    pairs = columns // 2
    assert batch == 1 and channels == 320 and rows % 8 == 0
    mean_scale = 1.0 / (micro_count * batch * replicas)
    chunk = hidden_width // replicas
    spread = chunk % 16 == 0 and replicas <= 8
    grad_shape = (
        jax.ShapeDtypeStruct((chunk, channels), F32)
        if spread
        else jax.ShapeDtypeStruct((hidden_width, channels), BF16)
    )
    others = max(replicas - 1, 1) if spread else 1
    slots = replicas if spread else 1
    vmem = pl.BlockSpec(memory_space=pltpu.VMEM)
    hbm = pl.BlockSpec(memory_space=pl.ANY)
    native = (micro_count, rows, width)
    stored, in_grad, out_grad, kernel_grad, gain_grad = pl.pallas_call(
        functools.partial(step_kernel, sections, replicas, spread, channels, mean_scale),
        out_shape=(
            jax.ShapeDtypeStruct(native, BF16),
            grad_shape,
            grad_shape,
            jax.ShapeDtypeStruct((KS * KS, channels), F32),
            jax.ShapeDtypeStruct((1, channels), F32),
        ),
        in_specs=[hbm, hbm, vmem, vmem, vmem, vmem],
        out_specs=(vmem,) * 5,
        scratch_shapes=[
            pltpu.VMEM(native, BF16),
            pltpu.VMEM(native, BF16),
            pltpu.VMEM(native, BF16),
            pltpu.VMEM((hidden_width, 384), BF16),
            pltpu.VMEM((hidden_width, 384), BF16),
            pltpu.VMEM((5, KS * KS, 8, LANES), F32),
            pltpu.VMEM((56, 384), F32),
            pltpu.VMEM((8, 384), F32),
            pltpu.VMEM((micro_count, pixels, hidden_width), BF16),
            pltpu.VMEM((micro_count, pixels, hidden_width), F32),
            pltpu.VMEM((micro_count, pixels, hidden_width), BF16),
            pltpu.VMEM((micro_count, pixels, 384), BF16),
            pltpu.VMEM((micro_count, pixels, 384), BF16),
            pltpu.VMEM((micro_count, pixels, 384), F32),
            pltpu.VMEM((micro_count, pixels, LANES), F32),
            pltpu.VMEM((micro_count, 5, pairs + 2 * REACH, rows + 16, LANES), F32),
            pltpu.VMEM((micro_count, 5, pairs, rows, LANES), F32),
            pltpu.VMEM((5, pairs, rows, LANES), F32),
            pltpu.VMEM((5, KS * KS, 8, LANES), F32),
            pltpu.VMEM((8, 384), F32),
            pltpu.VMEM((2, hidden_width, channels), BF16),
            pltpu.VMEM((2, others, chunk if spread else 16, channels), BF16),
            pltpu.VMEM((80, 384), BF16),
            pltpu.VMEM((slots, 80, 384), BF16),
            pltpu.SemaphoreType.DMA((2, micro_count)),
            pltpu.SemaphoreType.DMA((micro_count,)),
            pltpu.SemaphoreType.DMA((micro_count,)),
            pltpu.SemaphoreType.DMA((micro_count,)),
            pltpu.SemaphoreType.DMA((micro_count,)),
            pltpu.SemaphoreType.DMA((2, others)),
            pltpu.SemaphoreType.DMA((2, others)),
            pltpu.SemaphoreType.DMA((others,)),
            pltpu.SemaphoreType.DMA((others,)),
        ],
        compiler_params=pltpu.CompilerParams(
            collective_id=0, has_side_effects=True, vmem_limit_bytes=58 * 1024 * 1024
        ),
    )(
        images.reshape(native),
        cotangent.reshape(native),
        in_weight[0],
        out_weight[0],
        depth_kernel[0],
        norm_gain,
    )
    if not spread:
        in_grad, out_grad = (
            lax.psum_scatter(grad, "dp", scatter_dimension=0, tiled=True).astype(F32)
            for grad in (in_grad, out_grad)
        )
        kernel_grad, gain_grad = (
            lax.psum(grad.astype(BF16), "dp").astype(F32) for grad in (kernel_grad, gain_grad)
        )
    return (
        stored.reshape((1,) + images.shape),
        in_grad[None],
        out_grad[None],
        kernel_grad[None],
        gain_grad,
    )


def solution(mesh):
    placed = (
        P(None, ("groups", "dp"), None, None),
        P(None, ("groups", "dp"), None, None),
        P("section", None, None),
        P("section", None, None),
        P("section", None, None),
        P("section", None),
    )
    return jax.shard_map(
        local,
        mesh=mesh,
        in_specs=placed,
        out_specs=(
            P("section", None, ("groups", "dp"), None, None),
            P(("groups", "section"), "dp", None),
            P(("groups", "section"), "dp", None),
            P(("groups", "section"), None, None),
            P(("groups", "section"), None),
        ),
        check_vma=False,
    )
```

profile of v0, /device:TPU:0, one launch (start us, length us, event | category | flops | bytes accessed | tf_op | source)
XLA Modules:
  0.0 130.1 jit_solution(2840968072078678781)
XLA Ops:
  0.6 1.5 %copy.17 = f32[1,49,320]{2,1,0:T(8,128)} copy(f32[1,49,320]{2,0,1:T(1,128)} %param.10) | data formatting | bytes 125440
  2.2 0.0 copy-start
  2.2 2.3 %copy.11 = bf16[1,1280,320]{2,1,0:T(8,128)(2,1)} copy(bf16[1,1280,320]{1,2,0:T(8,128)(2,1)} %param.8) | data formatting | bytes 1638400 | tf_op args[2]
  4.4 0.0 copy-done
  4.4 1.3 copy.12
  5.7 118.2 %shard_map.101 = (bf16[4,16,5120]{2,1,0:T(8,128)(2,1)}, f32[320,320]{1,0:T(8,128)}, f32[320,320]{1,0:T(8,128)}, f32[49,320]{1,0:T(8,128)}, f32[1,320]{1,0:T(1,128)}) custom-call(bf16[4,16,5120]{2,1,0:T(8,128)(2,1)} %bitcast.16, bf16[4,16,5120]{2,1,0:T(8,128)(2,1)} %bitcast.17, bf16[1280,320]{1,0:T(8,128)(2,1)} %bitcast.13, bf16[1280,320]{1,0:T(8,128)(2,1)} %bitcast.14, ...), custom_call_target="tpu_custom_call" | custom-call | tf_op jit(solution)/shard_map/pallas_call | solution.py:426
  123.9 1.6 %copy.14 = f32[1,49,320]{2,0,1:T(1,128)} copy(f32[1,49,320]{2,1,0:T(8,128)} %bitcast.21) | data formatting | bytes 125440
  125.5 0.0 copy-start.2
  125.5 2.0 %copy.22 = bf16[1,4,1,16,5120]{4,3,2,1,0:T(8,128)(2,1)} copy(bf16[1,4,1,16,5120]{4,3,2,1,0:T(8,128)(2,1)} %bitcast.15) | data formatting | bytes 1310720
  127.5 0.0 copy-done.2
  127.5 0.0 copy-start.1
  127.6 0.8 copy.23
  128.3 0.4 copy-done.1
  128.8 0.0 copy-start.3
  128.8 0.8 copy.24
  129.5 0.0 copy-done.3
  129.5 0.6 copy.25
Async XLA Ops:
  2.2 2.3 %copy-start = (bf16[1,1280,320]{1,2,0:T(8,128)(2,1)S(1)}, bf16[1,1280,320]{1,2,0:T(8,128)(2,1)}, u32[]{:S(2)}) copy-start(bf16[1,1280,320]{1,2,0:T(8,128)(2,1)} %param.9) | copy-start | bytes 2457604
  125.5 2.0 %copy-start.2 = (f32[320,320]{1,0:T(8,128)S(1)}, f32[320,320]{1,0:T(8,128)}, u32[]{:S(2)}) copy-start(f32[320,320]{1,0:T(8,128)} %get-tuple-element.11) | copy-start | bytes 1228804
  127.5 1.2 copy-start.1
  128.8 0.8 copy-start.3
where the time goes:
time: 130 us
  Pallas kernels  118 us (91%)
  local copies, waits for them, and re-layouts  11.3 us (9%)
    pallas_call x1, Pallas kernels, local(): pl.pallas_call(functools.partial(step_kernel, sections, replicas, spread,...  118 us
    unnamed x16, local copies, waits for them, and re-layouts  11.3 us

commit v1 on v0

--- a/solution.py
+++ b/solution.py
@@ -146,13 +146,13 @@
     x_in, x_out, g_in, win, wout, taps, wide, gain_wide,
     hidden, slope, act_grad, normed, upstream, unit, inv_std,
     field, kept, conv, tap_sums, gain_sums, sent, landed, small, small_in,
-    load_sem, fwd_send, fwd_recv, bwd_send, bwd_recv, sum_send, sum_recv, small_send, small_recv,
+    load_sem, weight_sem, fwd_send, fwd_recv, bwd_send, bwd_recv, sum_send, sum_recv, small_send, small_recv,
 ):
     me = lax.axis_index("section")
     replica = lax.axis_index("dp")
     last = sections - 1
     micro_count, rows, width = x_in.shape
-    hidden_width = weight_in.shape[0]
+    hidden_width = weight_in.shape[1]
     step = 256
     chunks = hidden_width // step
     pixels = rows * (width // channels)
@@ -177,6 +177,13 @@
     def load(source, target, m, which):
         return pltpu.make_async_copy(source.at[m], target.at[m], load_sem.at[which, m])
 
+    weight_copies = tuple(
+        pltpu.make_async_copy(source, target.at[0:channels, :], weight_sem.at[k])
+        for k, (source, target) in enumerate(((weight_in, win), (weight_out, wout)))
+    )
+    for copy in weight_copies:
+        copy.start()
+
     for m in range(micro_count):
         @pl.when(me == 0)
         def _():
@@ -186,13 +193,12 @@
         def _():
             load(cotangent, g_in, m, 1).start()
 
-    win[:, 256:384] = jnp.zeros((hidden_width, 128), BF16)
-    wout[:, 256:384] = jnp.zeros((hidden_width, 128), BF16)
-    win[:, 0:channels] = weight_in[...]
-    wout[:, 0:channels] = weight_out[...]
+    win[channels:384, :] = jnp.zeros((384 - channels, hidden_width), BF16)
+    wout[channels:384, :] = jnp.zeros((384 - channels, hidden_width), BF16)
     wide[...] = jnp.zeros(wide.shape, F32)
     gain_wide[...] = jnp.zeros(gain_wide.shape, F32)
-    wide[0 : KS * KS, 0:channels] = kernel[...]
+    for t in range(KS * KS):
+        wide[t : t + 1, 0:channels] = kernel[t]
     gain_wide[:, 0:channels] = jnp.broadcast_to(gain[...], (8, channels))
     row_tiles = lane_tiles(wide[...])
     for k, tile in enumerate(merge_pair(row_tiles, row_tiles)):
@@ -203,6 +209,8 @@
     gain_sums[...] = jnp.zeros(gain_sums.shape, F32)
     gain_row = gain_wide[0:1, :]
 
+    for copy in weight_copies:
+        copy.wait()
     neighbours = jnp.where(me > 0, 1, 0) + jnp.where(me < last, 1, 0)
     if spread:
         neighbours = neighbours + replicas - 1
@@ -252,7 +260,7 @@
         mixed = None
         for c in range(chunks):
             at = slice(c * step, (c + 1) * step)
-            a = lax.dot_general(n, win[at, :], by_channel, preferred_element_type=F32)
+            a = jnp.dot(n, win[:, at], preferred_element_type=F32)
             square = a * a
             t = jnp.tanh(a * (gelu_scale + (gelu_scale * cubic_term) * square))
             plus = 0.5 + 0.5 * t
@@ -261,7 +269,7 @@
             slope[m, :, at] = plus + (a * (plus * (1.0 - t))) * (
                 gelu_scale + (3.0 * gelu_scale * cubic_term) * square
             )
-            term = jnp.dot(h, wout[at, :], preferred_element_type=F32)
+            term = lax.dot_general(h, wout[:, at], by_channel, preferred_element_type=F32)
             mixed = term if mixed is None else mixed + term
 
         @pl.when(me < last)
@@ -288,10 +296,10 @@
         dn = None
         for c in range(chunks):
             at = slice(c * step, (c + 1) * step)
-            hg = lax.dot_general(gb, wout[at, :], by_channel, preferred_element_type=F32)
+            hg = jnp.dot(gb, wout[:, at], preferred_element_type=F32)
             da = (hg * slope[m, :, at]).astype(BF16)
             act_grad[m, :, at] = da
-            term = jnp.dot(da, win[at, :], preferred_element_type=F32)
+            term = lax.dot_general(da, win[:, at], by_channel, preferred_element_type=F32)
             dn = term if dn is None else dn + term
         nhat = unit[m]
         along = dn * nhat
@@ -311,47 +319,115 @@
 
     lax.fori_loop(0, micro_count, backward, 0)
 
-    def share(w, k):
-        chunk = hidden_width // replicas
-        dest = lax.rem(replica + k, replicas)
+    half_chunk = hidden_width // replicas // 2
+
+    def rows_of(dest):
+        return pl.ds(pl.multiple_of(dest * half_chunk, 16), half_chunk)
+
+    def stage_of(way, t):
+        place = replica if way == 0 else replicas - 1 - replica
+        far = replicas - 1 - t + place
+        dest = far if way == 0 else replicas - 1 - far
+        return place, jnp.clip(dest, 0, replicas - 1)
+
+    def hop(way, w, dest, fresh):
+        target = replica + 1 if way == 0 else replica - 1
         return pltpu.make_async_remote_copy(
-            src_ref=sent.at[w, pl.ds(pl.multiple_of(dest * chunk, 16), chunk), :],
-            dst_ref=landed.at[w, k - 1],
-            send_sem=sum_send.at[w, k - 1], recv_sem=sum_recv.at[w, k - 1],
-            device_id={"dp": dest}, device_id_type=MESH,
+            src_ref=sent.at[w, rows_of(dest), :] if fresh else landed.at[way, w, dest],
+            dst_ref=landed.at[way, w, dest],
+            send_sem=sum_send.at[way, w, dest], recv_sem=sum_recv.at[way, w, dest],
+            device_id={"dp": jnp.clip(target, 0, replicas - 1)}, device_id_type=MESH,
         )
 
+    def stage(w, t):
+        for way in range(2):
+            place, dest = stage_of(way, t)
+            if t > 0:
+                settle(way, w, t - 1)
+
+            @pl.when(place == 0)
+            def _():
+                hop(way, w, dest, True).start()
+
+            @pl.when(jnp.logical_and(place > 0, place <= t))
+            def _():
+                onward = hop(way, w, dest, False)
+                onward.wait_recv()
+                slot = landed.at[way, w, dest]
+                own = sent[w, rows_of(dest), :]
+                slot[...] = (slot[...].astype(F32) + own.astype(F32)).astype(BF16)
+                onward.start()
+
+    def settle(way, w, t):
+        place, dest = stage_of(way, t)
+
+        @pl.when(place <= t)
+        def _():
+            hop(way, w, dest, False).wait_send()
+
+    def finish(w, target):
+        for way, there in ((0, replica > 0), (1, replica < replicas - 1)):
+
+            @pl.when(there)
+            def _():
+                hop(way, w, replica, False).wait_recv()
+                own = sent.at[w, rows_of(replica), :]
+                own[...] = (own[...].astype(F32) + landed[way, w, replica].astype(F32)).astype(BF16)
+
+            settle(way, w, replicas - 2)
+        first, second = split_pair(lane_tiles(sent[w, rows_of(replica), :].astype(F32)))
+        target[0:half_chunk, :] = jnp.concatenate(first, axis=1)[:, 0:channels]
+        target[half_chunk:, :] = jnp.concatenate(second, axis=1)[:, 0:channels]
+
     for w, (wide_side, thin_side) in enumerate(((hidden, upstream), (act_grad, normed))):
-        for c in range(chunks):
-            at = slice(c * step, (c + 1) * step)
-            total = lax.dot_general(
-                wide_side[:, :, at].reshape(micro_count * pixels, step),
-                thin_side[...].reshape(micro_count * pixels, 384),
-                by_pixel, preferred_element_type=F32,
-            )
-            total = (total[:, 0:channels] * mean_scale).astype(BF16)
-            if spread:
-                sent[w, at, :] = total
-            elif w == 0:
-                out_grad[at, :] = total
-            else:
-                in_grad[at, :] = total
+        total = jnp.concatenate(
+            [
+                lax.dot_general(
+                    wide_side[:, :, c * step : (c + 1) * step].reshape(micro_count * pixels, step),
+                    thin_side[...].reshape(micro_count * pixels, 384),
+                    by_pixel, preferred_element_type=F32,
+                )
+                for c in range(chunks)
+            ],
+            axis=0,
+        ) * mean_scale
         if spread:
-            for k in range(1, replicas):
-                share(w, k).start()
+            for dest in range(replicas):
+                at = 2 * dest * half_chunk
+                tiles = merge_pair(
+                    lane_tiles(total[at : at + half_chunk]),
+                    lane_tiles(total[at + half_chunk : at + 2 * half_chunk]),
+                )
+                for k, tile in enumerate(tiles):
+                    sent[
+                        w, dest * half_chunk : (dest + 1) * half_chunk, k * LANES : (k + 1) * LANES
+                    ] = tile.astype(BF16)
+            stage(w, 0)
+        elif w == 0:
+            out_grad[...] = total[:, 0:channels].astype(BF16)
+        else:
+            in_grad[...] = total[:, 0:channels].astype(BF16)
 
     def per_micro(m, carry):
         tap_terms(field, m, kept, tap_sums)
         return carry
 
-    lax.fori_loop(0, micro_count, per_micro, 0)
+    done = 0
+    if spread:
+        for t in range(1, replicas - 1):
+            lax.fori_loop(done, min(t, micro_count), per_micro, 0)
+            done = min(t, micro_count)
+            for w in range(2):
+                stage(w, t)
+    lax.fori_loop(done, micro_count, per_micro, 0)
 
     sums = tuple(jnp.sum(tap_sums[k], axis=1) for k in range(5))
     first, second = split_pair(sums)
     both = (jnp.concatenate(first, axis=1) + jnp.concatenate(second, axis=1)) * mean_scale
     gains = jnp.sum(gain_sums[...], axis=0, keepdims=True) * mean_scale
     if not spread:
-        kernel_grad[...] = both[:, 0:channels]
+        for t in range(KS * KS):
+            kernel_grad[t] = both[t : t + 1, 0:channels]
         gain_grad[...] = gains[:, 0:channels]
     else:
         small[...] = jnp.zeros(small.shape, BF16)
@@ -370,21 +446,15 @@
         for k in range(1, replicas):
             share_small(k).start()
         small_in[replica] = small[...]
-        chunk = hidden_width // replicas
-        mine = pl.ds(pl.multiple_of(replica * chunk, 16), chunk)
-        for w, target in ((0, out_grad), (1, in_grad)):
-            for k in range(1, replicas):
-                share(w, k).wait()
-            total = sent[w, mine, :].astype(F32)
-            for k in range(1, replicas):
-                total = total + landed[w, k - 1].astype(F32)
-            target[...] = total
+        finish(0, out_grad)
+        finish(1, in_grad)
         for k in range(1, replicas):
             share_small(k).wait()
         total = small_in[0].astype(F32)
         for k in range(1, replicas):
             total = total + small_in[k].astype(F32)
-        kernel_grad[...] = total[0 : KS * KS, 0:channels]
+        for t in range(KS * KS):
+            kernel_grad[t] = total[t : t + 1, 0:channels]
         gain_grad[...] = total[64:65, 0:channels]
 
     def drain(m, carry):
@@ -412,11 +482,9 @@
     assert batch == 1 and channels == 320 and rows % 8 == 0
     mean_scale = 1.0 / (micro_count * batch * replicas)
     chunk = hidden_width // replicas
-    spread = chunk % 16 == 0 and replicas <= 8
+    spread = chunk % 32 == 0 and 1 < replicas <= 8
     grad_shape = (
-        jax.ShapeDtypeStruct((chunk, channels), F32)
-        if spread
-        else jax.ShapeDtypeStruct((hidden_width, channels), BF16)
+        ((chunk, channels), F32) if spread else ((hidden_width, channels), BF16)
     )
     others = max(replicas - 1, 1) if spread else 1
     slots = replicas if spread else 1
@@ -426,20 +494,20 @@
     stored, in_grad, out_grad, kernel_grad, gain_grad = pl.pallas_call(
         functools.partial(step_kernel, sections, replicas, spread, channels, mean_scale),
         out_shape=(
-            jax.ShapeDtypeStruct(native, BF16),
-            grad_shape,
-            grad_shape,
-            jax.ShapeDtypeStruct((KS * KS, channels), F32),
-            jax.ShapeDtypeStruct((1, channels), F32),
+            pltpu.VMEM(native, BF16),
+            pltpu.VMEM(*grad_shape),
+            pltpu.VMEM(*grad_shape),
+            pltpu.VMEM((KS * KS, 1, channels), F32),
+            pltpu.VMEM((1, channels), F32),
         ),
-        in_specs=[hbm, hbm, vmem, vmem, vmem, vmem],
+        in_specs=[hbm, hbm, hbm, hbm, vmem, vmem],
         out_specs=(vmem,) * 5,
         scratch_shapes=[
             pltpu.VMEM(native, BF16),
             pltpu.VMEM(native, BF16),
             pltpu.VMEM(native, BF16),
-            pltpu.VMEM((hidden_width, 384), BF16),
-            pltpu.VMEM((hidden_width, 384), BF16),
+            pltpu.VMEM((384, hidden_width), BF16),
+            pltpu.VMEM((384, hidden_width), BF16),
             pltpu.VMEM((5, KS * KS, 8, LANES), F32),
             pltpu.VMEM((56, 384), F32),
             pltpu.VMEM((8, 384), F32),
@@ -455,31 +523,33 @@
             pltpu.VMEM((5, pairs, rows, LANES), F32),
             pltpu.VMEM((5, KS * KS, 8, LANES), F32),
             pltpu.VMEM((8, 384), F32),
-            pltpu.VMEM((2, hidden_width, channels), BF16),
-            pltpu.VMEM((2, others, chunk if spread else 16, channels), BF16),
+            pltpu.VMEM((2, hidden_width // 2, 2 * channels), BF16),
+            pltpu.VMEM((2, 2, slots, chunk // 2 if spread else 16, 2 * channels), BF16),
             pltpu.VMEM((80, 384), BF16),
             pltpu.VMEM((slots, 80, 384), BF16),
             pltpu.SemaphoreType.DMA((2, micro_count)),
+            pltpu.SemaphoreType.DMA((2,)),
             pltpu.SemaphoreType.DMA((micro_count,)),
             pltpu.SemaphoreType.DMA((micro_count,)),
             pltpu.SemaphoreType.DMA((micro_count,)),
             pltpu.SemaphoreType.DMA((micro_count,)),
-            pltpu.SemaphoreType.DMA((2, others)),
-            pltpu.SemaphoreType.DMA((2, others)),
+            pltpu.SemaphoreType.DMA((2, 2, slots)),
+            pltpu.SemaphoreType.DMA((2, 2, slots)),
             pltpu.SemaphoreType.DMA((others,)),
             pltpu.SemaphoreType.DMA((others,)),
         ],
         compiler_params=pltpu.CompilerParams(
-            collective_id=0, has_side_effects=True, vmem_limit_bytes=58 * 1024 * 1024
+            collective_id=0, has_side_effects=True, vmem_limit_bytes=52 * 1024 * 1024
         ),
     )(
         images.reshape(native),
         cotangent.reshape(native),
-        in_weight[0],
-        out_weight[0],
-        depth_kernel[0],
+        jnp.swapaxes(in_weight[0], 0, 1),
+        jnp.swapaxes(out_weight[0], 0, 1),
+        jnp.swapaxes(depth_kernel, 0, 1),
         norm_gain,
     )
+    kernel_grad = jnp.swapaxes(kernel_grad, 0, 1)
     if not spread:
         in_grad, out_grad = (
             lax.psum_scatter(grad, "dp", scatter_dimension=0, tiled=True).astype(F32)
@@ -492,7 +562,7 @@
         stored.reshape((1,) + images.shape),
         in_grad[None],
         out_grad[None],
-        kernel_grad[None],
+        kernel_grad,
         gain_grad,
     )
 

time: 130 us -> 106 us (0.82)
  Pallas kernels: 118 us -> 99.8 us
  local copies, waits for them, and re-layouts: 11.3 us -> 5.15 us
    pallas_call x1, Pallas kernels: 118 us -> 99.8 us  [local(): pl.pallas_call(functools.partial(step_kernel, sections, replicas, spread,...]
    unnamed x16 -> x9, local copies, waits for them, and re-layouts: 11.3 us -> 5.15 us
where the time goes in v1:
time: 106 us
  Pallas kernels  99.8 us (94%)
  local copies, waits for them, and re-layouts  5.15 us (5%)
    pallas_call x1, Pallas kernels, local(): pl.pallas_call(functools.partial(step_kernel, sections, replicas, spread,...  99.8 us
    unnamed x9, local copies, waits for them, and re-layouts  5.15 us

profile of v1, /device:TPU:0, one launch (start us, length us, event | category | flops | bytes accessed | tf_op | source)
XLA Modules:
  0.0 105.6 jit_solution(6468794974846625316)
XLA Ops:
  0.6 0.0 copy-start.1
  0.6 0.7 copy-done.1
  1.3 0.0 copy-start
  1.3 0.9 copy-done
  2.2 99.8 %shard_map.101 = (bf16[4,16,5120]{2,1,0:T(8,128)(2,1)S(1)}, f32[320,320]{1,0:T(8,128)S(1)}, f32[320,320]{1,0:T(8,128)S(1)}, f32[49,1,320]{2,1,0:T(1,128)S(1)}, f32[1,320]{1,0:T(1,128)S(1)}) custom-call(bf16[4,16,5120]{2,1,0:T(8,128)(2,1)} %bitcast.22, bf16[4,16,5120]{2,1,0:T(8,128)(2,1)} %bitcast.23, bf16[320,1280]{1,0:T(8,128)(2,1)} %bitcast.20, ...), custom_call_target="tpu_custom_call" | custom-call | tf_op jit(solution)/shard_map/pallas_call | solution.py:494
  102.0 0.8 copy.17
  102.9 0.8 copy.18
  103.6 0.6 copy.21
  104.2 0.6 copy.20
  104.8 0.8 copy.19
Async XLA Ops:
  0.6 0.7 copy-start.1
  1.3 0.9 copy-start

commit v2 on v1

--- a/solution.py
+++ b/solution.py
@@ -95,15 +95,14 @@
     pairs, rows = out.shape[1], out.shape[2]
 
     def one_tile(k, carry):
-        for part in range(rows // 8):
-            total = jnp.zeros((pairs, 8, LANES), F32)
-            for i in range(KS):
-                window = field[slot, k, :, 8 - REACH + i + 8 * part : 16 - REACH + i + 8 * part, :]
-                for j in range(KS):
-                    tap = KS * i + j
-                    tap = KS * KS - 1 - tap if flip else tap
-                    total = total + window[j : j + pairs] * taps[k, tap][None]
-            out[k, :, 8 * part : 8 * part + 8, :] = total
+        total = jnp.zeros((pairs, rows, LANES), F32)
+        for i in range(KS):
+            window = field[slot, k, :, 8 - REACH + i : 8 - REACH + i + rows, :]
+            for j in range(KS):
+                tap = KS * i + j
+                tap = KS * KS - 1 - tap if flip else tap
+                total = total + window[j : j + pairs] * taps[k, tap][0:1][None]
+        out[k] = total
         return carry
 
     lax.fori_loop(0, 5, one_tile, 0)

time: 106 us -> 106 us (level)
  no operation moved by 1% of the time
where the time goes in v2:
time: 106 us
  Pallas kernels  100 us (94%)
  local copies, waits for them, and re-layouts  5.15 us (5%)
    pallas_call x1, Pallas kernels, local(): pl.pallas_call(functools.partial(step_kernel, sections, replicas, spread,...  100 us
    unnamed x9, local copies, waits for them, and re-layouts  5.15 us

profile of v2, /device:TPU:0, one launch (start us, length us, event | category | flops | bytes accessed | tf_op | source)
XLA Modules:
  0.0 105.8 jit_solution(17961296362302663287)
XLA Ops:
  0.6 0.0 copy-start.1
  0.6 0.7 copy-done.1
  1.3 0.0 copy-start
  1.3 0.9 copy-done
  2.2 100.0 %shard_map.101 = (bf16[4,16,5120]{2,1,0:T(8,128)(2,1)S(1)}, f32[320,320]{1,0:T(8,128)S(1)}, f32[320,320]{1,0:T(8,128)S(1)}, f32[49,1,320]{2,1,0:T(1,128)S(1)}, f32[1,320]{1,0:T(1,128)S(1)}) custom-call(bf16[4,16,5120]{2,1,0:T(8,128)(2,1)} %bitcast.22, bf16[4,16,5120]{2,1,0:T(8,128)(2,1)} %bitcast.23, bf16[320,1280]{1,0:T(8,128)(2,1)} %bitcast.20, ...), custom_call_target="tpu_custom_call" | custom-call | tf_op jit(solution)/shard_map/pallas_call | solution.py:493
  102.2 0.8 copy.17
  103.1 0.8 copy.18
  103.9 0.6 copy.21
  104.4 0.6 copy.20
  105.1 0.8 copy.19
Async XLA Ops:
  0.6 0.7 copy-start.1
  1.3 0.9 copy-start
